TPU v7x, 32 devices: a whole 2x2x4 slice. The times are simulated.
32 devices in a mesh: seq: 16 (over z, x, core), head: 2 (over y).
Axes of the slice: x: 2, y: 2, z: 4, core: 2. Of those that a mesh axis runs over, the one named last changes fastest.
Arguments:
- queries: bfloat16 [16384, 5120], P(('seq', 'head')), may hold values from -7.5 to 7.5
- keys: bfloat16 [16384, 1024], P(('seq', 'head')), may hold values from -7.5 to 7.5
- values: bfloat16 [16384, 1024], P(('seq', 'head')), may hold values from -6 to 6
- fetch_list: int32 [16, 16, 2], replicated, may hold values from 0 to 15, as said below
- choose: int32 [256, 16], P('seq'), may hold values from 0 to 31, as said below
- live: int32 [256], P('seq'), may hold values from 0 to 16, as said below
Outputs:
- attn_out: bfloat16 [16384, 5120], P(('seq', 'head'))
Inputs may be any that keep to these rules, and one draw needn't show every extreme that they name: Each row fetch_list[d, s] holds 2 distinct blocks. Each row of choose holds 16 distinct slots; slot j stands for entry j % 2 of fetch_list[d, j // 2]; the first live[b] entries of row b name slots j with j // 2 < b // 16. live[b] is at most 2 * (b // 16); every draw has a block with live equal to 16.
All inputs are finite; a program needn't handle non-finite values.
Results may differ from a plain program's by a relative error of at most 0.0042.
Values may be sent and summed in bfloat16 or wider, within the bound.
No kernel may reach another device: no remote copies, remote signals or barrier semaphores. Data moves between devices by JAX's collectives and lax.ppermute only.
A program may use at most 64 MiB of HBM per device.

v0:
```python
import math

import jax
import jax.numpy as jnp
from jax import lax
from jax.sharding import PartitionSpec as P

HEAD_WIDTH = 128
BLOCK_TOKENS = 64
LISTED_ENTRIES = 16


def normalize(scores):
    highest = jnp.max(scores, axis=-1, keepdims=True)
    weights = jnp.exp(scores - highest)
    totals = jnp.sum(weights, axis=-1)
    return (weights.astype(jnp.bfloat16), totals)


def body(queries, keys, values, fetch_list, choose, live):
    scaling = 1.0 / math.sqrt(HEAD_WIDTH)
    q_all, k_all, v_all = (
        lax.all_to_all(queries, "head", split_axis=1, concat_axis=0, tiled=True),
        lax.all_to_all(keys, "head", split_axis=1, concat_axis=0, tiled=True),
        lax.all_to_all(values, "head", split_axis=1, concat_axis=0, tiled=True),
    )
    tokens_here = q_all.shape[0]
    kv_heads = k_all.shape[1] // HEAD_WIDTH
    q_heads = q_all.shape[1] // HEAD_WIDTH
    repeat_factor = q_heads // kv_heads
    blocks_here = tokens_here // BLOCK_TOKENS
    position = lax.axis_index("seq")
    wanted = lax.dynamic_index_in_dim(fetch_list, position, 1, keepdims=False)
    k_rows = k_all.reshape(blocks_here, BLOCK_TOKENS * kv_heads * HEAD_WIDTH)
    v_rows = v_all.reshape(blocks_here, BLOCK_TOKENS * kv_heads * HEAD_WIDTH)
    send_k = k_rows[wanted]
    send_v = v_rows[wanted]
    got_k, got_v = (
        lax.all_to_all(send_k, "seq", split_axis=0, concat_axis=0, tiled=True),
        lax.all_to_all(send_v, "seq", split_axis=0, concat_axis=0, tiled=True),
    )
    slot_count = got_k.shape[0] * got_k.shape[1]
    got_k = got_k.reshape(slot_count, BLOCK_TOKENS, kv_heads, HEAD_WIDTH)
    got_v = got_v.reshape(slot_count, BLOCK_TOKENS, kv_heads, HEAD_WIDTH)
    group_blocks = 1
    while group_blocks * BLOCK_TOKENS * q_heads < 512 and blocks_here % (2 * group_blocks) == 0:
        group_blocks = group_blocks * 2
    group_count = blocks_here // group_blocks
    q_groups = q_all.reshape(
        group_count, group_blocks, BLOCK_TOKENS, kv_heads, repeat_factor, HEAD_WIDTH
    )
    k_groups = k_all.reshape(group_count, group_blocks, BLOCK_TOKENS, kv_heads, HEAD_WIDTH)
    v_groups = v_all.reshape(group_count, group_blocks, BLOCK_TOKENS, kv_heads, HEAD_WIDTH)
    c_groups = choose.reshape(group_count, group_blocks, LISTED_ENTRIES)
    l_groups = live.reshape(group_count, group_blocks)

    def one_group(inputs):
        q_block, own_k, own_v, picked, counts = inputs
        imp_k = got_k[picked]
        imp_v = got_v[picked]
        keys_all = jnp.concatenate([own_k[:, None], imp_k], axis=1).reshape(
            group_blocks, (LISTED_ENTRIES + 1) * BLOCK_TOKENS, kv_heads, HEAD_WIDTH
        )
        vals_all = jnp.concatenate([own_v[:, None], imp_v], axis=1).reshape(
            group_blocks, (LISTED_ENTRIES + 1) * BLOCK_TOKENS, kv_heads, HEAD_WIDTH
        )
        scores = (
            jnp.einsum("bqhgd,bkhd->bhgqk", q_block, keys_all, preferred_element_type=jnp.float32)
            * scaling
        )
        column = jnp.arange((LISTED_ENTRIES + 1) * BLOCK_TOKENS, dtype=jnp.int32)
        query_row = jnp.arange(BLOCK_TOKENS, dtype=jnp.int32)
        key_block = column // BLOCK_TOKENS
        own_ok = ((key_block == 0)[None, :] & (column[None, :] <= query_row[:, None]))[None]
        import_ok = (key_block >= 1)[None, None, :] & (
            key_block[None, None, :] <= counts[:, None, None]
        )
        allowed = own_ok | import_ok
        scores = jnp.where(allowed[:, None, None], scores, -jnp.inf)
        rounded, totals = normalize(scores)
        mixed = jnp.einsum(
            "bhgqk,bkhd->bqhgd", rounded, vals_all, preferred_element_type=jnp.float32
        )
        result = mixed / jnp.transpose(totals, (0, 3, 1, 2))[..., None]
        return result.astype(jnp.bfloat16)

    outputs = lax.map(one_group, (q_groups, k_groups, v_groups, c_groups, l_groups))
    attended = outputs.reshape(tokens_here, q_heads * HEAD_WIDTH)
    return lax.all_to_all(attended, "head", split_axis=0, concat_axis=1, tiled=True)


def solution(mesh):
    placed = (
        P(("seq", "head"), None),
        P(("seq", "head"), None),
        P(("seq", "head"), None),
        P(),
        P("seq", None),
        P("seq"),
    )
    return jax.shard_map(
        body, mesh=mesh, in_specs=placed, out_specs=P(("seq", "head"), None), check_vma=False
    )
```

profile of v0, /device:TPU:0, one launch (start us, length us, event | category | flops | bytes accessed | tf_op | source)
XLA Modules:
  0.0 647.5 jit_solution(2565964385833936209)
XLA Ops:
  2.4 4.2 all-to-all-start
  7.7 13.4 %all-to-all-done = bf16[512,2,512]{2,0,1:T(8,128)(2,1)S(1)} async-done(((bf16[512,2,512]{2,0,1:T(8,128)(2,1)}), bf16[512,2,512]{2,0,1:T(8,128)(2,1)S(1)}, u32[]{:S(2)}, u32[]{:S(2)}) %all-to-all-start) | async-done | bytes 1048608 | tf_op jit(solution)/shard_map/all_to_all | solution.py:25
  21.0 3.6 all-to-all-start.2
  24.6 5.2 copy.68
  29.9 8.1 %all-to-all-done.2 = bf16[512,2,512]{2,0,1:T(8,128)(2,1)S(1)} async-done(((bf16[512,2,512]{2,0,1:T(8,128)(2,1)}), bf16[512,2,512]{2,0,1:T(8,128)(2,1)S(1)}, u32[]{:S(2)}, u32[]{:S(2)}) %all-to-all-start.2) | async-done | bytes 1048608 | tf_op jit(solution)/shard_map/all_to_all | solution.py:24
  37.9 6.0 all-to-all-start.4
  44.9 3.2 gather_fusion.2
  48.1 4.4 reshape.306
  52.5 48.9 %all-to-all-done.4 = bf16[512,2,2560]{2,0,1:T(8,128)(2,1)} async-done(((bf16[512,2,2560]{2,0,1:T(8,128)(2,1)}), bf16[512,2,2560]{2,0,1:T(8,128)(2,1)}, u32[]{:S(2)}, u32[]{:S(2)}) %all-to-all-start.4) | async-done | bytes 5242912 | tf_op jit(solution)/shard_map/all_to_all | solution.py:23
  101.4 5.5 all-to-all-start.1
  107.5 3.2 gather_fusion.3
  110.7 4.4 reshape.314
  115.1 33.0 %all-to-all-done.1 = bf16[16,2,32768]{2,1,0:T(2,128)(2,1)} async-done(((bf16[16,2,32768]{2,1,0:T(2,128)(2,1)}), bf16[16,2,32768]{2,1,0:T(2,128)(2,1)}, u32[]{:S(2)}, u32[]{:S(2)}) %all-to-all-start.1) | async-done | bytes 2097184 | tf_op jit(solution)/shard_map/all_to_all | solution.py:40
  148.1 11.3 %all-to-all-start.3 = ((bf16[16,2,32768]{2,1,0:T(2,128)(2,1)}), bf16[16,2,32768]{2,1,0:T(2,128)(2,1)}, u32[]{:S(2)}, u32[]{:S(2)}) async-start(bf16[16,2,32768]{2,1,0:T(2,128)(2,1)} %reshape.314), calls=%async_computation.3 | async-start | bytes 4194304 | tf_op jit(solution)/shard_map/all_to_all | solution.py:39
  164.6 12.8 %reshape.288 = bf16[16,1,64,4,5,128]{5,4,3,2,0,1:T(8,128)(2,1)} reshape(bf16[2,512,2560]{2,1,0:T(8,128)(2,1)} %bitcast.26) | data formatting | bytes 10485760 | tf_op jit(solution)/shard_map/reshape | solution.py:49
  177.4 9.4 %copy.55 = bf16[16,1,64,4,5,128]{5,2,4,3,1,0:T(8,128)(2,1)} copy(bf16[16,1,64,4,5,128]{5,4,3,2,0,1:T(8,128)(2,1)} %reshape.288) | data formatting | bytes 10485760 | tf_op jit(solution)/shard_map/while | solution.py:87
  186.8 4.5 reshape.283
  191.4 9.2 %all-to-all-done.3 = bf16[16,2,32768]{2,1,0:T(2,128)(2,1)} async-done(((bf16[16,2,32768]{2,1,0:T(2,128)(2,1)}), bf16[16,2,32768]{2,1,0:T(2,128)(2,1)}, u32[]{:S(2)}, u32[]{:S(2)}) %all-to-all-start.3) | async-done | bytes 2097184 | tf_op jit(solution)/shard_map/all_to_all | solution.py:39
  200.5 4.5 reshape.287
  205.1 335.8 %while.12 = (s32[]{:T(128)}, bf16[16,1,64,4,5,128]{5,2,4,3,1,0:T(8,128)(2,1)}, bf16[16,1,64,4,128]{4,2,1,3,0:T(8,128)(2,1)S(1)}, s32[16,1,16]{2,1,0:T(1,128)}, b...) while((s32[]{:T(128)}, ...), condition=%wide.region_3.4_spmd, body=%wide.region_0.3_spmd.sunk | while | flops 724442432 | bytes 59943640 | solution.py:87
  207.6 3.0 gather_fusion.1
  217.5 3.0 gather_fusion
  221.6 4.5 fusion.55
  228.6 3.0 gather_fusion.1
  238.5 3.0 gather_fusion
  242.6 4.5 fusion.55
  249.6 3.0 gather_fusion.1
  259.5 3.0 gather_fusion
  263.6 4.5 fusion.55
  270.5 3.0 gather_fusion.1
  284.6 4.5 fusion.55
  305.5 4.5 fusion.55
  326.5 4.5 fusion.55
  347.5 4.5 fusion.55
  368.5 4.5 fusion.55
  389.5 4.5 fusion.55
  410.5 4.5 fusion.55
  431.5 4.5 fusion.55
  452.5 4.5 fusion.55
  473.5 4.5 fusion.55
  494.5 4.5 fusion.55
  515.4 4.5 fusion.55
  536.4 4.5 fusion.55
  540.9 10.0 %copy.56 = bf16[16,1,64,4,5,128]{5,4,3,2,0,1:T(8,128)(2,1)} copy(bf16[16,1,64,4,5,128]{5,2,4,3,1,0:T(8,128)(2,1)} %get-tuple-element.119) | data formatting | bytes 10485760 | tf_op jit(solution)/shard_map/while | solution.py:87
  550.9 12.6 %all_to_all.67 = bf16[2,512,2560]{2,1,0:T(8,128)(2,1)} reshape(bf16[16,1,64,4,5,128]{5,4,3,2,0,1:T(8,128)(2,1)} %copy.56) | data formatting | bytes 10485760 | tf_op jit(solution)/shard_map/all_to_all | solution.py:89
  563.6 68.2 %all_to_all.77 = bf16[2,512,2560]{2,1,0:T(8,128)(2,1)} all-to-all(bf16[2,512,2560]{2,1,0:T(8,128)(2,1)} %all_to_all.67), channel_id=1, replica_groups=mesh['seq'=16,'head'=2] {'head'}, dimensions={0} | all-to-all | bytes 10485760 | tf_op jit(solution)/shard_map/all_to_all | solution.py:89
  631.8 7.8 %copy.57 = bf16[512,2,2560]{0,2,1:T(8,128)(2,1)} copy(bf16[512,2,2560]{2,0,1:T(8,128)(2,1)} %bitcast.126) | data formatting | bytes 10485760 | tf_op jit(solution)/shard_map/all_to_all | solution.py:89
  639.6 7.9 %copy.58 = bf16[512,5120]{1,0:T(8,128)(2,1)} copy(bf16[512,5120]{0,1:T(8,128)(2,1)} %bitcast.127) | data formatting | bytes 10485760 | tf_op jit(solution)/shard_map/all_to_all | solution.py:89
  (304 shorter events, 251.7 us)
Async XLA Ops:
  0.0 44.0 %copy-start = (s32[16,16,2]{1,2,0:T(2,128)S(1)}, s32[16,16,2]{1,2,0:T(2,128)}, u32[]{:S(2)}) copy-start(s32[16,16,2]{1,2,0:T(2,128)} %param.11) | copy-start | bytes 6148
  0.0 6.6 %copy-start.3 = (bf16[512,1024]{1,0:T(8,128)(2,1)S(1)}, bf16[512,1024]{1,0:T(8,128)(2,1)}, u32[]{:S(2)}) copy-start(bf16[512,1024]{1,0:T(8,128)(2,1)} %param.9) | copy-start | bytes 3145732
  2.4 18.7 %all-to-all-start = ((bf16[512,2,512]{2,0,1:T(8,128)(2,1)}), bf16[512,2,512]{2,0,1:T(8,128)(2,1)S(1)}, u32[]{:S(2)}, u32[]{:S(2)}) async-start(bf16[512,2,512]{2,0,1:T(8,128)(2,1)} %bitcast.92), calls=%async_computation | async-start | bytes 2097152 | tf_op jit(solution)/shard_map/all_to_all | solution.py:25
  21.0 16.9 %all-to-all-start.2 = ((bf16[512,2,512]{2,0,1:T(8,128)(2,1)}), bf16[512,2,512]{2,0,1:T(8,128)(2,1)S(1)}, u32[]{:S(2)}, u32[]{:S(2)}) async-start(bf16[512,2,512]{2,0,1:T(8,128)(2,1)} %bitcast.91), calls=%async_computation.2 | async-start | bytes 2097152 | tf_op jit(solution)/shard_map/all_to_all | solution.py:24
  37.9 63.4 %all-to-all-start.4 = ((bf16[512,2,2560]{2,0,1:T(8,128)(2,1)}), bf16[512,2,2560]{2,0,1:T(8,128)(2,1)}, u32[]{:S(2)}, u32[]{:S(2)}) async-start(bf16[512,2,2560]{2,0,1:T(8,128)(2,1)} %bitcast.125), calls=%async_computation.4 | async-start | bytes 10485760 | tf_op jit(solution)/shard_map/all_to_all | solution.py:23
  101.4 46.7 %all-to-all-start.1 = ((bf16[16,2,32768]{2,1,0:T(2,128)(2,1)}), bf16[16,2,32768]{2,1,0:T(2,128)(2,1)}, u32[]{:S(2)}, u32[]{:S(2)}) async-start(bf16[16,2,32768]{2,1,0:T(2,128)(2,1)} %reshape.306), calls=%async_computation.1 | async-start | bytes 4194304 | tf_op jit(solution)/shard_map/all_to_all | solution.py:40
  148.1 52.4 %all-to-all-start.3 = ((bf16[16,2,32768]{2,1,0:T(2,128)(2,1)}), bf16[16,2,32768]{2,1,0:T(2,128)(2,1)}, u32[]{:S(2)}, u32[]{:S(2)}) async-start(bf16[16,2,32768]{2,1,0:T(2,128)(2,1)} %reshape.314), calls=%async_computation.3 | async-start | bytes 4194304 | tf_op jit(solution)/shard_map/all_to_all | solution.py:39
  191.4 13.7 %copy-start.4 = (s32[16]{0:T(128)S(1)}, s32[16]{0:T(128)}, u32[]{:S(2)}) copy-start(s32[16]{0:T(128)} %param.13) | copy-start | bytes 196
  215.0 2.5 copy-start.2
  236.0 2.5 copy-start.2
  257.0 2.5 copy-start.2
  278.0 2.5 copy-start.2
  299.0 2.5 copy-start.2
  319.9 2.5 copy-start.2
  340.9 2.5 copy-start.2
  361.9 2.5 copy-start.2
  382.9 2.5 copy-start.2
  403.9 2.5 copy-start.2
  424.9 2.5 copy-start.2
  445.9 2.5 copy-start.2
  466.9 2.5 copy-start.2
  487.9 2.5 copy-start.2
  508.9 2.5 copy-start.2
  529.8 2.5 copy-start.2
  639.6 7.9 %copy-start.1 = (s32[16,16,2]{1,2,0:T(2,128)S(1)}, s32[16,16,2]{1,2,0:T(2,128)}, u32[]{:S(2)}) copy-start(s32[16,16,2]{1,2,0:T(2,128)} %param.11) | copy-start | bytes 6148
where the time goes:
time: 657 us; the launch traced here: 648 us
  local copies, waits for them, and re-layouts  268 us (41%)
  waiting for transfers between devices  112 us (17%)
  matrix products  106 us (16%)
  blocking collectives  68.2 us (10%)
  other arithmetic  60.6 us (9%)
  starting transfers between devices  30.6 us (5%)
    dot_general x16, matrix products, one_group(): jnp.einsum('bhgqk,bkhd->bqhgd', rounded, vals_all, preferred_element_type...  71.3 us
    all_to_all x1, blocking collectives, body(): lax.all_to_all(attended, 'head', split_axis=0, concat_axis=1, tiled=True)  68.2 us
    all_to_all x1, waiting for transfers between devices, body(): lax.all_to_all(queries, 'head', split_axis=1, concat_axis=0, tiled=True)  48.9 us
    gather x16, local copies, waits for them, and re-layouts, one_group(): imp_k = got_k[picked]  48.6 us
    gather x16, local copies, waits for them, and re-layouts, one_group(): imp_v = got_v[picked]  48.6 us
    dot_general x16, matrix products, one_group(): jnp.einsum('bqhgd,bkhd->bhgqk', q_block, keys_all, preferred_element_type...  34.6 us
    all_to_all x1, waiting for transfers between devices, body(): lax.all_to_all(send_v, 'seq', split_axis=0, concat_axis=0, tiled=True)  33 us
    another operation x32, local copies, waits for them, and re-layouts  28.4 us
  transfers between devices with their start and end apart: 5, of which 5 were waited for; matrix products, arithmetic and copies ran while one was open for 8% of the time, Pallas kernels for 0%

commit v1 on v0

v1 whole, which is shorter than its diff:
```python
import functools
import math

import jax
import jax.numpy as jnp
from jax import lax
from jax.experimental import pallas as pl
from jax.experimental.pallas import tpu as pltpu
from jax.sharding import PartitionSpec as P

HEAD_WIDTH = 128
BLOCK_TOKENS = 64
LISTED_ENTRIES = 16
CAP = 2
STEP_BLOCKS = 4
MASKED = -1e30
NEAR = 4
ATTEND_FLOPS = 6 * 10**9
ROW_ORDER = (1, 2, 3)
VMEM_BYTES = 60 * 2**20
ANY = pl.BlockSpec(memory_space=pl.ANY)
SMEM = pl.BlockSpec(memory_space=pltpu.SMEM)


def entries(rows_of):
    return [(a, m) for a in range(rows_of) for m in range(NEAR) if (a, m) != (0, 0)]


def count_of(form, rows_of):
    return {"shard": 1, "place": NEAR, "row": rows_of}[form]


def lengths_of(form, rows_of):
    if form == "place":
        return [rows_of - (m == 0) for m in range(NEAR)]
    return [NEAR - (a == 0) for a in range(rows_of)]


def entry_of(form, arrays, ahead, m):
    if form == "place":
        return arrays[m].at[ahead - (m == 0)]
    return arrays[ahead].at[m - (ahead == 0)]


def pick_kernel(shape, place, wanted, keys, values, *refs):
    planes, n_seq, form, tokens, local_heads, first, group_heads, after_n = shape
    rows_of, near = n_seq // NEAR, NEAR
    others, outs = refs[: planes - 1], refs[planes - 1 + after_n : -3]
    shard, load_sems, sems = refs[-3:]
    seq, head = place[0], place[1]
    lanes = group_heads * HEAD_WIDTH
    column = pl.multiple_of((head * local_heads + first) * HEAD_WIDTH, HEAD_WIDTH)

    def part(plane):
        return pl.ds(pl.multiple_of(plane * tokens, tokens), tokens)

    loads = []
    for which, source in enumerate((keys, values)):
        loads.append((source.at[:, pl.ds(column, lanes)], shard.at[which, part(head)]))
    for turn in range(1, planes):
        loads.append((others[turn - 1], shard.at[:, part(lax.rem(head + turn, planes))]))
    loads = [pltpu.make_async_copy(*ends, load_sems.at[i]) for i, ends in enumerate(loads)]
    for copy in loads:
        copy.start()
    for copy in loads:
        copy.wait()

    def each(h, dest, out, act):
        columns = slice(h * HEAD_WIDTH, (h + 1) * HEAD_WIDTH)
        for entry in range(CAP):
            row = pl.multiple_of(wanted[dest, entry] * BLOCK_TOKENS, BLOCK_TOKENS)
            source = shard.at[:, pl.ds(row, BLOCK_TOKENS), columns]
            into = out.at[:, pl.ds(entry * BLOCK_TOKENS, BLOCK_TOKENS)]
            act(pltpu.make_async_copy(source, into, sems.at[h, dest, entry]))

    def all_of(act):
        for h in range(group_heads):
            if form == "shard":

                @pl.loop(seq + 1, n_seq)
                def _(dest):
                    each(h, dest, outs[h].at[dest], act)

            else:
                mine = outs[h * len(outs) // group_heads :]
                for ahead, m in entries(rows_of):
                    dest = (seq // near + ahead) * near + jnp.bitwise_xor(seq % near, m)

                    @pl.when((dest > seq) & (dest < n_seq))
                    def _():
                        each(h, dest, entry_of(form, mine, ahead, m), act)

    all_of(lambda copy: copy.start())
    all_of(lambda copy: copy.wait())


def regroup_kernel(shape, place, *refs):
    n_seq, form, into, back = shape
    rows_of = n_seq // NEAR
    n_in, n_out = count_of(form, rows_of), count_of(into, rows_of)
    ins, outs, bufs = refs[:n_in], refs[n_in : n_in + n_out], refs[n_in + n_out : -2]
    load_sems, sems = refs[-2:]
    row = place[0] // NEAR
    loads = [pltpu.make_async_copy(ins[i], bufs[i], load_sems.at[i]) for i in range(n_in)]

    def stores(act):
        for ahead, m in entries(rows_of):

            @pl.when((row - ahead >= 0) if back else (row + ahead < rows_of))
            def _():
                ends = entry_of(form, bufs, ahead, m), entry_of(into, outs, ahead, m)
                act(pltpu.make_async_copy(*ends, sems.at[ahead, m]))

    for copy in loads:
        copy.start()
    for copy in loads:
        copy.wait()
    stores(lambda copy: copy.start())
    stores(lambda copy: copy.wait())


def attend_scratch(n_seq, tokens, group_heads, repeat):
    blocks_here = tokens // BLOCK_TOKENS
    rows, columns = repeat * BLOCK_TOKENS, STEP_BLOCKS * BLOCK_TOKENS
    steps = LISTED_ENTRIES // STEP_BLOCKS + 1
    units = group_heads * blocks_here * steps + 4
    return [
        pltpu.VMEM((group_heads, tokens, repeat * HEAD_WIDTH), jnp.bfloat16),
        pltpu.VMEM(
            (group_heads, 2, (n_seq * CAP + blocks_here) * BLOCK_TOKENS, HEAD_WIDTH), jnp.bfloat16
        ),
        pltpu.VMEM((group_heads, tokens, repeat * HEAD_WIDTH), jnp.bfloat16),
        pltpu.VMEM((rows, columns), jnp.float32),
        pltpu.VMEM((rows, columns), jnp.bfloat16),
        pltpu.VMEM((rows, HEAD_WIDTH), jnp.float32),
        pltpu.VMEM((rows, HEAD_WIDTH), jnp.float32),
        pltpu.VMEM((rows, HEAD_WIDTH), jnp.float32),
        pltpu.VMEM((rows, HEAD_WIDTH), jnp.float32),
        pltpu.SMEM((units, 4), jnp.int32),
        pltpu.SMEM((units, STEP_BLOCKS), jnp.int32),
        pltpu.SemaphoreType.DMA((group_heads, 3)),
        pltpu.SemaphoreType.DMA((n_seq, group_heads)),
        pltpu.SemaphoreType.DMA((group_heads, blocks_here)),
    ]


def attend_kernel(shape, place, choose, live, queries, keys, values, *refs):
    n_seq, n_head, local_heads, repeat, jobs, aliased = shape
    group_heads = len(jobs)
    pieces = []
    for _, plane, _, form in jobs:
        count = count_of(form, n_seq // NEAR)
        pieces.append((form, refs[:count] if form != "shard" else [refs[0].at[plane]]))
        refs = refs[count:]
    refs = refs[1 if aliased else 0 :]
    out, q_buf, kv_buf, o_buf, scores, weights, acc, top, total, shrink = refs[:10]
    units, taken, sems, piece_sems, out_sems = refs[10:]
    tokens = q_buf.shape[1]
    blocks_here = tokens // BLOCK_TOKENS
    seq, head = place[0], place[1]
    first_block = head * blocks_here
    slots = n_seq * CAP
    q_lanes = repeat * HEAD_WIDTH
    piece_rows = CAP * BLOCK_TOKENS
    own_rows = pl.ds(slots * BLOCK_TOKENS, tokens)
    columns = STEP_BLOCKS * BLOCK_TOKENS
    rows = repeat * BLOCK_TOKENS

    def kv_head(h):
        whose, plane, at, _ = jobs[h]
        return (lax.rem(head + plane, n_head) if whose == "turn" else plane) * local_heads + at

    q_heads = [kv_head(h) for h in range(group_heads)]

    loads = []
    for h in range(group_heads):
        q_cols = pl.ds(pl.multiple_of(q_heads[h] * q_lanes, HEAD_WIDTH), q_lanes)
        kv_cols = pl.ds(pl.multiple_of(q_heads[h] * HEAD_WIDTH, HEAD_WIDTH), HEAD_WIDTH)
        loads += [
            pltpu.make_async_copy(queries.at[:, q_cols], q_buf.at[h], sems.at[h, 0]),
            pltpu.make_async_copy(keys.at[:, kv_cols], kv_buf.at[h, 0, own_rows], sems.at[h, 1]),
            pltpu.make_async_copy(values.at[:, kv_cols], kv_buf.at[h, 1, own_rows], sems.at[h, 2]),
        ]

    def piece_do(h, source, piece, act):
        into = pl.ds(pl.multiple_of(source * piece_rows, piece_rows), piece_rows)
        act(pltpu.make_async_copy(piece, kv_buf.at[h, :, into], piece_sems.at[source, h]))

    def pieces_do(act):
        for h, (form, arrays) in enumerate(pieces):
            if form == "shard":

                @pl.loop(0, seq)
                def _(source):
                    piece_do(h, source, arrays[0].at[source], act)

            else:
                for behind, m in entries(n_seq // NEAR):
                    source = (seq // NEAR - behind) * NEAR + jnp.bitwise_xor(seq % NEAR, m)

                    @pl.when((source >= 0) & (source < seq))
                    def _():
                        piece_do(h, source, entry_of(form, arrays, behind, m), act)

    for copy in loads:
        copy.start()
    pieces_do(lambda copy: copy.start())

    def put(unit, h, block, at, last):
        units[unit, 0] = h
        units[unit, 1] = block
        units[unit, 2] = at
        units[unit, 3] = last
        count = live[first_block + block]
        for i in range(STEP_BLOCKS):
            entry = at * STEP_BLOCKS + i
            slot = choose[first_block + block, jnp.clip(entry - 1, 0, LISTED_ENTRIES - 1)]
            dead = (entry == 0) | (entry > count)
            taken[unit, i] = jnp.where(dead, slots + block, slot) * BLOCK_TOKENS

    put(0, 0, 0, 0, 0)
    put(1, 0, 0, 0, 0)

    def put_block(i, at_unit):
        h, block = i // blocks_here, i % blocks_here
        steps = (live[first_block + block] + STEP_BLOCKS) // STEP_BLOCKS

        @pl.loop(0, steps)
        def _(at):
            put(at_unit + at, h, block, at, jnp.where(at == steps - 1, 1, 0))

        return at_unit + steps

    last_unit = lax.fori_loop(0, group_heads * blocks_here, put_block, jnp.int32(2))
    put(last_unit, 0, 0, 0, 0)
    put(last_unit + 1, 0, 0, 0, 0)

    scores[...] = jnp.zeros_like(scores)
    weights[...] = jnp.zeros_like(weights)
    for buf in (acc, top, total, shrink):
        buf[...] = jnp.zeros_like(buf)

    for copy in loads:
        copy.wait()
    pieces_do(lambda copy: copy.wait())

    factor = math.log2(math.e) / math.sqrt(HEAD_WIDTH)
    column = lax.broadcasted_iota(jnp.int32, (BLOCK_TOKENS, columns), 1)
    row = lax.broadcasted_iota(jnp.int32, (BLOCK_TOKENS, columns), 0)

    def block_rows(block):
        return pl.ds(pl.multiple_of(block * BLOCK_TOKENS, BLOCK_TOKENS), BLOCK_TOKENS)

    def out_copy(h, block):
        at = block_rows(block)
        q_head = q_heads[0]
        for i in range(1, group_heads):
            q_head = jnp.where(h == i, q_heads[i], q_head)
        q_cols = pl.ds(pl.multiple_of(q_head * q_lanes, HEAD_WIDTH), q_lanes)
        return pltpu.make_async_copy(o_buf.at[h, at], out.at[at, q_cols], out_sems.at[h, block])

    def gathered(unit, which):
        h = units[unit, 0]
        parts = []
        for i in range(STEP_BLOCKS):
            at = pl.ds(pl.multiple_of(taken[unit, i], BLOCK_TOKENS), BLOCK_TOKENS)
            parts.append(kv_buf[h, which, at, :])
        return jnp.concatenate(parts, axis=0)

    def turn(unit, carry):
        oldest = unit - 2
        mixed = jnp.dot(weights[...], gathered(oldest, 1), preferred_element_type=jnp.float32)
        mixed = acc[...] * shrink[...] + mixed
        acc[...] = mixed
        result = (mixed * (1.0 / total[...])).astype(jnp.bfloat16)
        h, at = units[oldest, 0], block_rows(units[oldest, 1])
        for r in range(repeat):
            o_buf[h, at, r * HEAD_WIDTH : (r + 1) * HEAD_WIDTH] = result[
                r * BLOCK_TOKENS : (r + 1) * BLOCK_TOKENS
            ]

        before = unit - 1
        at_step = units[before, 2]
        count = live[first_block + units[before, 1]]
        limit = (count + 1 - at_step * STEP_BLOCKS) * BLOCK_TOKENS
        reach = jnp.where(at_step == 0, 0, columns)
        allowed = (column < limit) & ((column >= BLOCK_TOKENS) | (column <= row + reach))
        old = jnp.where(at_step == 0, MASKED, top[...])
        kept = jnp.where(
            allowed[None], scores[...].reshape(repeat, BLOCK_TOKENS, columns), MASKED
        ).reshape(rows, columns)
        high = jnp.maximum(jnp.max(kept, axis=-1, keepdims=True), old)
        fade = jnp.exp2((old - high) * factor)
        parts = [
            jnp.exp2((kept[:, i : i + HEAD_WIDTH] - high) * factor)
            for i in range(0, columns, HEAD_WIDTH)
        ]
        sums = jnp.sum(functools.reduce(jnp.add, parts), axis=-1, keepdims=True)
        for i, part in enumerate(parts):
            weights[:, i * HEAD_WIDTH : (i + 1) * HEAD_WIDTH] = part.astype(jnp.bfloat16)
        top[...] = high
        shrink[...] = fade
        total[...] = total[...] * fade + sums

        h, at = units[unit, 0], block_rows(units[unit, 1])
        q = jnp.concatenate(
            [q_buf[h, at, r * HEAD_WIDTH : (r + 1) * HEAD_WIDTH] for r in range(repeat)], axis=0
        )
        scores[...] = lax.dot_general(
            q, gathered(unit, 0), (((1,), (1,)), ((), ())), preferred_element_type=jnp.float32
        )

        @pl.when(units[oldest, 3] == 1)
        def _():
            out_copy(units[oldest, 0], units[oldest, 1]).start()

        return carry

    lax.fori_loop(2, last_unit + 2, turn, 0)

    for h in range(group_heads):

        @pl.loop(0, blocks_here)
        def _(block):
            out_copy(h, block).wait()


def body(queries, keys, values, fetch_list, choose, live, *, n_seq, n_head):
    tokens, q_width = queries.shape
    kv_heads = keys.shape[1] // HEAD_WIDTH
    repeat = q_width // HEAD_WIDTH // kv_heads
    local_heads = kv_heads // n_head
    rows_of = n_seq // NEAR
    seq, head = lax.axis_index("seq"), lax.axis_index("head")
    wanted = lax.dynamic_index_in_dim(fetch_list, seq, 1, keepdims=False)
    place = jnp.stack([seq, head]).astype(jnp.int32)

    def piece(*lead):
        return jax.ShapeDtypeStruct(lead + (2, CAP * BLOCK_TOKENS, HEAD_WIDTH), jnp.bfloat16)

    def exchange(first, heads):
        others = []
        for turn in range(1, n_head):
            theirs = lax.rem(head + n_head - turn, n_head) * local_heads + first
            part = jnp.stack(
                [
                    lax.dynamic_slice_in_dim(x, theirs * HEAD_WIDTH, heads * HEAD_WIDTH, axis=1)
                    for x in (keys, values)
                ]
            )
            back = [(h, (h + n_head - turn) % n_head) for h in range(n_head)]
            others.append(lax.ppermute(part, "head", back))
        return others

    def pick(first, heads, form, others, after=()):
        if form == "shard":
            shapes = [piece(n_seq)] * heads
        else:
            shapes = [piece(n) for n in lengths_of(form, rows_of)] * heads
        outs = pl.pallas_call(
            functools.partial(
                pick_kernel,
                (n_head, n_seq, form, tokens, local_heads, first, heads, len(after)),
            ),
            out_shape=shapes,
            in_specs=[SMEM, SMEM] + [ANY] * (2 + len(others) + len(after)),
            out_specs=[ANY] * len(shapes),
            scratch_shapes=[
                pltpu.VMEM((2, n_head * tokens, heads * HEAD_WIDTH), jnp.bfloat16),
                pltpu.SemaphoreType.DMA((1 + n_head,)),
                pltpu.SemaphoreType.DMA((heads, n_seq, CAP)),
            ],
            compiler_params=pltpu.CompilerParams(vmem_limit_bytes=VMEM_BYTES),
            name="pick",
        )(place, wanted, keys, values, *others, *after)
        per_head = len(shapes) // heads
        return [outs[h * per_head : (h + 1) * per_head] for h in range(heads)]

    def regroup(form, into, back, parts):
        return pl.pallas_call(
            functools.partial(regroup_kernel, (n_seq, form, into, back)),
            out_shape=[piece(n) for n in lengths_of(into, rows_of)],
            in_specs=[SMEM] + [ANY] * len(parts),
            out_specs=[ANY] * count_of(into, rows_of),
            scratch_shapes=[pltpu.VMEM(part.shape, part.dtype) for part in parts]
            + [pltpu.SemaphoreType.DMA((len(parts),)), pltpu.SemaphoreType.DMA((rows_of, NEAR))],
            compiler_params=pltpu.CompilerParams(vmem_limit_bytes=VMEM_BYTES),
            name="regroup",
        )(place, *parts)

    def attend(jobs, out):
        aliased = out is not None
        operands = [place, choose, live, queries, keys, values]
        shapes = []
        for whose, plane, at, form, arrays in jobs:
            operands += arrays
            shapes.append((whose, plane, at, form))
        operands += [out] if aliased else []
        return pl.pallas_call(
            functools.partial(
                attend_kernel, (n_seq, n_head, local_heads, repeat, tuple(shapes), aliased)
            ),
            out_shape=jax.ShapeDtypeStruct(queries.shape, queries.dtype),
            in_specs=[SMEM] * 3 + [ANY] * (len(operands) - 3),
            out_specs=ANY,
            scratch_shapes=attend_scratch(n_seq, tokens, len(jobs), repeat),
            input_output_aliases={len(operands) - 1: 0} if aliased else {},
            compiler_params=pltpu.CompilerParams(vmem_limit_bytes=VMEM_BYTES),
            cost_estimate=pl.CostEstimate(
                flops=ATTEND_FLOPS * len(jobs), bytes_accessed=8 * 2**20, transcendentals=0
            ),
            name="attend",
        )(*operands)

    def over_rows(arrays):
        got = [arrays[0]] + [None] * (rows_of - 1)
        for ahead in ROW_ORDER:
            step = ahead * NEAR
            pairs = [(s, s + step) for s in range(n_seq - step)]
            got[ahead] = lax.ppermute(arrays[ahead], "seq", pairs)
        return got

    def in_row(arrays):
        return [arrays[0]] + [
            lax.ppermute(arrays[m], "seq", [(s, s ^ m) for s in range(n_seq)])
            for m in range(1, NEAR)
        ]

    def swap(arrays):
        return [lax.ppermute(x, "head", [(0, 1), (1, 0)]) for x in arrays]

    if n_head != 2 or rows_of != 4 or local_heads != 4:
        out = None
        for at in range(local_heads):
            sends = pick(at, 1, "shard", exchange(at, 1))[0]
            got = lax.all_to_all(sends[0], "seq", split_axis=0, concat_axis=0, tiled=True)
            whole = lax.all_gather(got, "head", axis=0, tiled=False)
            for plane in range(n_head):
                out = attend([("plane", plane, at, "shard", [whole])], out)
        return out

    first, second, rest = exchange(0, 1), exchange(1, 1), exchange(2, local_heads - 2)
    sent = over_rows(pick(0, 1, "row", first)[0])
    parts = in_row(pick(1, 1, "place", second)[0])
    grouped = regroup("place", "row", False, parts)
    imports = [None, ("row", over_rows(grouped))]
    picked = pick(2, local_heads - 2, "place", rest, [grouped[0]])
    imports[0] = ("place", in_row(regroup("row", "place", True, sent)))
    for sends in picked:
        imports.append(("row", over_rows(regroup("place", "row", False, in_row(sends)))))
    turned = [(form, swap(arrays)) for form, arrays in imports]
    out = None
    for at in range(local_heads + 1):
        jobs = []
        if at > 0:
            jobs.append(("turn", 1, at - 1) + turned[at - 1])
        if at < local_heads:
            jobs.append(("turn", 0, at) + imports[at])
        out = attend(jobs, out)
    return out


def solution(mesh):
    placed = (
        P(("seq", "head"), None),
        P(("seq", "head"), None),
        P(("seq", "head"), None),
        P(),
        P("seq", None),
        P("seq"),
    )
    return jax.shard_map(
        functools.partial(body, n_seq=mesh.shape["seq"], n_head=mesh.shape["head"]),
        mesh=mesh,
        in_specs=placed,
        out_specs=P(("seq", "head"), None),
        check_vma=False,
    )
```

time: 657 us -> 181 us (0.28); the launches traced: 648 us -> 180 us
  local copies, waits for them, and re-layouts: 268 us -> 8.09 us
  matrix products: 106 us -> 0 us
  waiting for transfers between devices: 112 us -> 29.5 us
  blocking collectives: 68.2 us -> 0 us
  other arithmetic: 60.6 us -> 0.75 us
  Pallas kernels: 0 us -> 57.3 us
  starting transfers between devices: 30.6 us -> 83.6 us
    all_to_all x5 -> x0, waiting for transfers between devices: 112 us -> none  [the longest x1 48.9 us: body(): lax.all_to_all(queries, 'head', split_axis=1, concat_axis=0, tiled=True)]
    gather x36 -> x0, local copies, waits for them, and re-layouts: 112 us -> none  [the longest x16 48.6 us: one_group(): imp_k = got_k[picked]]
    dot_general x32 -> x0, matrix products: 106 us -> none  [the longest x16 71.3 us: one_group(): jnp.einsum('bhgqk,bkhd->bqhgd', rounded, vals_all, preferred_element_type...]
    ppermute x0 -> x43, starting transfers between devices: none -> 83.6 us  [the longest x12 51 us: over_rows(): got[ahead] = lax.ppermute(arrays[ahead], 'seq', pairs)]
    all_to_all x1 -> x0, blocking collectives: 68.2 us -> none  [body(): lax.all_to_all(attended, 'head', split_axis=0, concat_axis=1, tiled=True)]
    pallas_call x0 -> x12, Pallas kernels: none -> 57.3 us  [the longest x5 35.3 us: attend(): pl.pallas_call(functools.partial(attend_kernel, (n_seq, n_head, local_hea...]
    while x36 -> x0, local copies, waits for them, and re-layouts: 45.8 us -> none
    all_to_all x6 -> x0, local copies, waits for them, and re-layouts: 37 us -> none  [the longest x3 28.4 us: body(): lax.all_to_all(attended, 'head', split_axis=0, concat_axis=1, tiled=True)]
  transfers between devices with their start and end apart: 5 -> 43, of which waited for: 5 -> 12; matrix products, arithmetic and copies ran while one was open for 8% -> 1% of each run, Pallas kernels for 0% -> 29%
where the time goes in v1:
time: 181 us; the launch traced here: 180 us
  starting transfers between devices  83.6 us (46%)
  Pallas kernels  57.3 us (32%)
  waiting for transfers between devices  29.5 us (16%)
  local copies, waits for them, and re-layouts  8.09 us (4%)
    ppermute x12, starting transfers between devices, over_rows(): got[ahead] = lax.ppermute(arrays[ahead], 'seq', pairs)  51 us
    pallas_call x5, Pallas kernels, attend(): pl.pallas_call(functools.partial(attend_kernel, (n_seq, n_head, local_hea...  35.3 us
    ppermute x16, starting transfers between devices, swap(): return [lax.ppermute(x, 'head', [(0, 1), (1, 0)]) for x in arrays]  19 us
    ppermute x16, waiting for transfers between devices, swap(): return [lax.ppermute(x, 'head', [(0, 1), (1, 0)]) for x in arrays]  17.5 us
    pallas_call x4, Pallas kernels, regroup(): pl.pallas_call(functools.partial(regroup_kernel, (n_seq, form, into, back...  11.8 us
    pallas_call x3, Pallas kernels, pick(): pl.pallas_call(functools.partial(pick_kernel, (n_head, n_seq, form, token...  10.3 us
    ppermute x12, starting transfers between devices, in_row(): lax.ppermute(arrays[m], 'seq', [(s, s ^ m) for s in range(n_seq)])  8.9 us
    unnamed x92, local copies, waits for them, and re-layouts  5.01 us
  transfers between devices with their start and end apart: 43, of which 12 were waited for; matrix products, arithmetic and copies ran while one was open for 1% of the time, Pallas kernels for 29%

profile of v1, /device:TPU:0, one launch (start us, length us, event | category | flops | bytes accessed | tf_op | source)
XLA Modules:
  0.0 179.9 jit_solution(5861215028802175187)
XLA Ops:
  0.0 1.2 dynamic-slice_bitcast_fusion.2
  1.2 3.0 %collective-permute-start.32 = (bf16[2,512,128]{2,1,0:T(8,128)(2,1)S(1)}, bf16[2,512,128]{2,1,0:T(8,128)(2,1)S(1)}, u32[]{:S(2)}, u32[]{:S(2)}) collective-permute-start(bf16[2,512,128]{2,1,0:T(8,128)(2,1)S(1)} %pad_maximum_fusion.2), channel_id=1, source_target_pairs={{0,1},{1,0},{2,3},{3,2},{4,5},{5,4},{6,7},{7,6},{8,9},{9,8},{10,11... | collective-permute-start | bytes 786440 | tf_op jit(solution)/shard_map/ppermute | solution.py:352
  6.9 4.4 %collective-permute-done.32.refs_0_ = bf16[2,512,128]{2,1,0:T(8,128)(2,1)S(1)} collective-permute-done((bf16[2,512,128]{2,1,0:T(8,128)(2,1)S(1)}, bf16[2,512,128]{2,1,0:T(8,128)(2,1)S(1)}, u32[]{:S(2)}, u32[]{:S(2)}) %collective-permute-start.32) | collective-permute-done | bytes 262176 | tf_op jit(solution)/shard_map/ppermute | solution.py:352
  12.1 3.2 %pick.5 = (bf16[3,2,128,128]{3,2,1,0:T(8,128)(2,1)}, bf16[4,2,128,128]{3,2,1,0:T(8,128)(2,1)}, bf16[4,2,128,128]{3,2,1,0:T(8,128)(2,1)}, bf16[4,2,128,128]{3,2,1,0:T(8,128)(2,1)}) custom-call(s32[2]{0:T(128)} %pad_add_fusion.place, s32[16,2]{1,0:T(8,128)} %copy.13.wanted, bf16[512,1024]{1,0:T(8,128)(2,1)} %keys.15, bf16[512,1024]{1,0:T(8,128)(2,1)} %values.15, ...), custom_call_target="tpu_custom_call" | custom-call | tf_op jit(solution)/shard_map/pick/pallas_call | solution.py:360
  15.3 3.9 %collective-permute-start.33 = (bf16[4,2,128,128]{3,2,1,0:T(8,128)(2,1)}, bf16[4,2,128,128]{3,2,1,0:T(8,128)(2,1)S(1)}, u32[]{:S(2)}, u32[]{:S(2)}) collective-permute-start(bf16[4,2,128,128]{3,2,1,0:T(8,128)(2,1)} %get-tuple-element.62), channel_id=1, source_target_pairs={{0,8},{2,10},{4,12},{6,14},{8,16},{10,18},{12,20},{14,22},{16,24},... | collective-permute-start | bytes 786440 | tf_op jit(solution)/shard_map/ppermute | solution.py:420
  19.2 4.3 %collective-permute-start.34 = (bf16[4,2,128,128]{3,2,1,0:T(8,128)(2,1)}, bf16[4,2,128,128]{3,2,1,0:T(8,128)(2,1)S(1)}, u32[]{:S(2)}, u32[]{:S(2)}) collective-permute-start(bf16[4,2,128,128]{3,2,1,0:T(8,128)(2,1)} %get-tuple-element.63), channel_id=1, source_target_pairs={{0,16},{2,18},{4,20},{6,22},{8,24},{10,26},{12,28},{14,30},{1,17},... | collective-permute-start | bytes 786440 | tf_op jit(solution)/shard_map/ppermute | solution.py:420
  23.6 1.6 collective-permute-start
  25.2 1.3 collective-permute-start.35
  27.2 3.2 %pick.3 = (bf16[3,2,128,128]{3,2,1,0:T(8,128)(2,1)}, bf16[4,2,128,128]{3,2,1,0:T(8,128)(2,1)}, bf16[4,2,128,128]{3,2,1,0:T(8,128)(2,1)}, bf16[4,2,128,128]{3,2,1,0:T(8,128)(2,1)}) custom-call(s32[2]{0:T(128)} %pad_add_fusion.place, s32[16,2]{1,0:T(8,128)} %copy.13.wanted, bf16[512,1024]{1,0:T(8,128)(2,1)} %keys.15, bf16[512,1024]{1,0:T(8,128)(2,1)} %values.15, ...), custom_call_target="tpu_custom_call" | custom-call | tf_op jit(solution)/shard_map/pick/pallas_call | solution.py:360
  30.4 1.5 collective-permute-start.3
  32.3 2.3 %collective-permute-done.35.refs_3_ = bf16[4,2,128,128]{3,2,1,0:T(8,128)(2,1)S(1)} collective-permute-done((bf16[4,2,128,128]{3,2,1,0:T(8,128)(2,1)}, bf16[4,2,128,128]{3,2,1,0:T(8,128)(2,1)S(1)}, u32[]{:S(2)}, u32[]{:S(2)}) %collective-permute-start.35) | collective-permute-done | bytes 262176 | tf_op jit(solution)/shard_map/ppermute | solution.py:420
  35.3 2.7 %regroup.7 = (bf16[3,2,128,128]{3,2,1,0:T(8,128)(2,1)}, bf16[4,2,128,128]{3,2,1,0:T(8,128)(2,1)}, bf16[4,2,128,128]{3,2,1,0:T(8,128)(2,1)}, bf16[4,2,128,128]{3,2,1,0:T(8,128)(2,1)}) custom-call(s32[2]{0:T(128)} %pad_add_fusion.place, bf16[3,2,128,128]{3,2,1,0:T(8,128)(2,1)} %get-tuple-element.61.refs_0_, bf16[4,2,128,128]{3,2,1,0:T(8,128)(2,1)} %copy-done.7, ...), custom_call_target="tpu_custom_call" | custom-call | tf_op jit(solution)/shard_map/regroup/pallas_call | solution.py:380
  38.2 1.6 collective-permute-start.39
  39.8 1.4 collective-permute-start.36
  41.2 3.2 %collective-permute-done.4.refs_3_ = bf16[4,2,128,128]{3,2,1,0:T(8,128)(2,1)S(1)} collective-permute-done((bf16[4,2,128,128]{3,2,1,0:T(8,128)(2,1)}, bf16[4,2,128,128]{3,2,1,0:T(8,128)(2,1)S(1)}, u32[]{:S(2)}, u32[]{:S(2)}) %collective-permute-start.4) | collective-permute-done | bytes 262176 | tf_op jit(solution)/shard_map/ppermute | solution.py:425
  45.2 3.0 %regroup.4 = (bf16[3,2,128,128]{3,2,1,0:T(8,128)(2,1)}, bf16[4,2,128,128]{3,2,1,0:T(8,128)(2,1)}, bf16[4,2,128,128]{3,2,1,0:T(8,128)(2,1)}, bf16[4,2,128,128]{3,2,1,0:T(8,128)(2,1)}) custom-call(s32[2]{0:T(128)} %pad_add_fusion.place, bf16[3,2,128,128]{3,2,1,0:T(8,128)(2,1)} %get-tuple-element.37.refs_0_, bf16[4,2,128,128]{3,2,1,0:T(8,128)(2,1)} %copy-done.6, ...), custom_call_target="tpu_custom_call" | custom-call | tf_op jit(solution)/shard_map/regroup/pallas_call | solution.py:380
  48.8 1.8 collective-permute-start.41
  50.6 3.9 %pick.4 = (bf16[3,2,128,128]{3,2,1,0:T(8,128)(2,1)}, bf16[4,2,128,128]{3,2,1,0:T(8,128)(2,1)}, bf16[4,2,128,128]{3,2,1,0:T(8,128)(2,1)}, bf16[4,2,128,128]{3,2,1...) custom-call(s32[2]{0:T(128)} %pad_add_fusion.place, ...), custom_call_target="tpu_custom_call" | custom-call | tf_op jit(solution)/shard_map/pick/pallas_call | solution.py:360
  54.5 8.6 %collective-permute-start.26 = (bf16[4,2,128,128]{3,2,1,0:T(8,128)(2,1)}, bf16[4,2,128,128]{3,2,1,0:T(8,128)(2,1)S(1)}, u32[]{:S(2)}, u32[]{:S(2)}) collective-permute-start(bf16[4,2,128,128]{3,2,1,0:T(8,128)(2,1)} %get-tuple-element.58), channel_id=1, source_target_pairs={{0,8},{2,10},{4,12},{6,14},{8,16},{10,18},{12,20},{14,22},{16,24},... | collective-permute-start | bytes 786440 | tf_op jit(solution)/shard_map/ppermute | solution.py:420
  65.2 5.7 %collective-permute-start.28 = (bf16[4,2,128,128]{3,2,1,0:T(8,128)(2,1)}, bf16[4,2,128,128]{3,2,1,0:T(8,128)(2,1)S(1)}, u32[]{:S(2)}, u32[]{:S(2)}) collective-permute-start(bf16[4,2,128,128]{3,2,1,0:T(8,128)(2,1)} %get-tuple-element.59), channel_id=1, source_target_pairs={{0,16},{2,18},{4,20},{6,22},{8,24},{10,26},{12,28},{14,30},{1,17},... | collective-permute-start | bytes 786440 | tf_op jit(solution)/shard_map/ppermute | solution.py:420
  70.9 4.9 %collective-permute-start.30 = (bf16[4,2,128,128]{3,2,1,0:T(8,128)(2,1)}, bf16[4,2,128,128]{3,2,1,0:T(8,128)(2,1)S(1)}, u32[]{:S(2)}, u32[]{:S(2)}) collective-permute-start(bf16[4,2,128,128]{3,2,1,0:T(8,128)(2,1)} %get-tuple-element.60), channel_id=1, source_target_pairs={{0,24},{2,26},{4,28},{6,30},{1,25},{3,27},{5,29},{7,31}} | collective-permute-start | bytes 786440 | tf_op jit(solution)/shard_map/ppermute | solution.py:420
  75.9 1.3 collective-permute-start.6
  78.0 3.0 %regroup.6 = (bf16[3,2,128,128]{3,2,1,0:T(8,128)(2,1)}, bf16[4,2,128,128]{3,2,1,0:T(8,128)(2,1)}, bf16[4,2,128,128]{3,2,1,0:T(8,128)(2,1)}, bf16[4,2,128,128]{3,2,1,0:T(8,128)(2,1)}) custom-call(s32[2]{0:T(128)} %pad_add_fusion.place, bf16[3,2,128,128]{3,2,1,0:T(8,128)(2,1)} %get-tuple-element.50.refs_0_, bf16[4,2,128,128]{3,2,1,0:T(8,128)(2,1)} %copy-done.5, ...), custom_call_target="tpu_custom_call" | custom-call | tf_op jit(solution)/shard_map/regroup/pallas_call | solution.py:380
  81.7 1.7 collective-permute-done.30.refs_7_
  83.4 8.2 %collective-permute-start.19 = (bf16[4,2,128,128]{3,2,1,0:T(8,128)(2,1)}, bf16[4,2,128,128]{3,2,1,0:T(8,128)(2,1)S(1)}, u32[]{:S(2)}, u32[]{:S(2)}) collective-permute-start(bf16[4,2,128,128]{3,2,1,0:T(8,128)(2,1)} %get-tuple-element.55), channel_id=1, source_target_pairs={{0,8},{2,10},{4,12},{6,14},{8,16},{10,18},{12,20},{14,22},{16,24},... | collective-permute-start | bytes 786440 | tf_op jit(solution)/shard_map/ppermute | solution.py:420
  91.6 5.3 %collective-permute-start.21 = (bf16[4,2,128,128]{3,2,1,0:T(8,128)(2,1)}, bf16[4,2,128,128]{3,2,1,0:T(8,128)(2,1)S(1)}, u32[]{:S(2)}, u32[]{:S(2)}) collective-permute-start(bf16[4,2,128,128]{3,2,1,0:T(8,128)(2,1)} %get-tuple-element.56), channel_id=1, source_target_pairs={{0,16},{2,18},{4,20},{6,22},{8,24},{10,26},{12,28},{14,30},{1,17},... | collective-permute-start | bytes 786440 | tf_op jit(solution)/shard_map/ppermute | solution.py:420
  96.9 1.6 collective-permute-start.38
  99.1 1.5 collective-permute-start.42
  100.6 5.5 %attend.5.refs_8_ = bf16[512,5120]{1,0:T(8,128)(2,1)} custom-call(s32[2]{0:T(128)} %pad_add_fusion.place, s32[16,16]{1,0:T(8,128)} %choose.9, s32[16]{0:T(128)} %live.9, bf16[512,5120]{1,0:T(8,128)(2,1)} %queries.9, bf16[512,1024]{1,0:T(8,128)(2,1)} %keys.15, bf16[512,1024]{1,0:T(8,128)(2,1)} %values.15, bf16[3,2,128,128]{3,2,1,0:T(8,128)(2,1)} %get-tuple-element.65.refs_0_, ...), custom_call_target="tpu_custom_call" | custom-call | flops 6000000000 | bytes 8388608 | tf_op jit(solution)/shard_map/attend/pallas_call | solution.py:399
  106.1 3.0 %regroup.5 = (bf16[3,2,128,128]{3,2,1,0:T(8,128)(2,1)}, bf16[4,2,128,128]{3,2,1,0:T(8,128)(2,1)}, bf16[4,2,128,128]{3,2,1,0:T(8,128)(2,1)}, bf16[4,2,128,128]{3,2,1,0:T(8,128)(2,1)}) custom-call(s32[2]{0:T(128)} %pad_add_fusion.place, bf16[3,2,128,128]{3,2,1,0:T(8,128)(2,1)} %get-tuple-element.42.refs_0_, bf16[4,2,128,128]{3,2,1,0:T(8,128)(2,1)} %copy-done.2, ...), custom_call_target="tpu_custom_call" | custom-call | tf_op jit(solution)/shard_map/regroup/pallas_call | solution.py:380
  109.1 1.3 collective-permute-start.23
  110.5 1.4 collective-permute-done.40.refs_2_
  111.9 2.9 %collective-permute-start.11 = (bf16[4,2,128,128]{3,2,1,0:T(8,128)(2,1)}, bf16[4,2,128,128]{3,2,1,0:T(8,128)(2,1)S(1)}, u32[]{:S(2)}, u32[]{:S(2)}) collective-permute-start(bf16[4,2,128,128]{3,2,1,0:T(8,128)(2,1)} %get-tuple-element.48), channel_id=1, source_target_pairs={{0,16},{2,18},{4,20},{6,22},{8,24},{10,26},{12,28},{14,30},{1,17},... | collective-permute-start | bytes 786440 | tf_op jit(solution)/shard_map/ppermute | solution.py:420
  115.8 1.5 collective-permute-start.27
  117.9 1.6 collective-permute-start.31
  119.5 8.1 %attend.6.refs_8_ = bf16[512,5120]{1,0:T(8,128)(2,1)} custom-call(s32[2]{0:T(128)} %pad_add_fusion.place, s32[16,16]{1,0:T(8,128)} %choose.9, s32[16]{0:T(128)} %live.9, bf16[512,5120]{1,0:T(8,128)(2,1)} %queries.9, bf16[512,1024]{1,0:T(8,128)(2,1)} %keys.15, bf16[512,1024]{1,0:T(8,128)(2,1)} %values.15, ...), custom_call_target="tpu_custom_call", output_to_operand_aliasing={{}: (14, {})} | custom-call | flops 12000000000 | bytes 8388608 | tf_op jit(solution)/shard_map/attend/pallas_call | solution.py:399
  127.7 1.5 collective-permute-start.13
  129.2 3.2 %collective-permute-start.9 = (bf16[4,2,128,128]{3,2,1,0:T(8,128)(2,1)S(1)}, bf16[4,2,128,128]{3,2,1,0:T(8,128)(2,1)S(1)}, u32[]{:S(2)}, u32[]{:S(2)}) collective-permute-start(bf16[4,2,128,128]{3,2,1,0:T(8,128)(2,1)S(1)} %copy-done.27), channel_id=1, source_target_pairs={{0,8},{2,10},{4,12},{6,14},{8,16},{10,18},{12,20},{14,22},{16,24},... | collective-permute-start | bytes 786440 | tf_op jit(solution)/shard_map/ppermute | solution.py:420
  132.4 2.7 %collective-permute-start.20 = (bf16[4,2,128,128]{3,2,1,0:T(8,128)(2,1)S(1)}, bf16[4,2,128,128]{3,2,1,0:T(8,128)(2,1)S(1)}, u32[]{:S(2)}, u32[]{:S(2)}) collective-permute-start(bf16[4,2,128,128]{3,2,1,0:T(8,128)(2,1)S(1)} %collective-permute-done.19.refs_5_), channel_id=1, source_target_pairs={{0,1},{1,0},{2,3},{3,2},{4,5},{5,4},{6,7},{7,6},{8,9},{9,8},{10,11... | collective-permute-start | bytes 786440 | tf_op jit(solution)/shard_map/ppermute | solution.py:430
  135.3 1.9 %collective-permute-start.24 = (bf16[4,2,128,128]{3,2,1,0:T(8,128)(2,1)S(1)}, bf16[4,2,128,128]{3,2,1,0:T(8,128)(2,1)S(1)}, u32[]{:S(2)}, u32[]{:S(2)}) collective-permute-start(bf16[4,2,128,128]{3,2,1,0:T(8,128)(2,1)S(1)} %collective-permute-done.23.refs_7_), channel_id=1, source_target_pairs={{0,1},{1,0},{2,3},{3,2},{4,5},{5,4},{6,7},{7,6},{8,9},{9,8},{10,11... | collective-permute-start | bytes 786440 | tf_op jit(solution)/shard_map/ppermute | solution.py:430
  137.2 8.1 %attend.7.refs_8_ = bf16[512,5120]{1,0:T(8,128)(2,1)} custom-call(s32[2]{0:T(128)} %pad_add_fusion.place, s32[16,16]{1,0:T(8,128)} %choose.9, s32[16]{0:T(128)} %live.9, bf16[512,5120]{1,0:T(8,128)(2,1)} %queries.9, bf16[512,1024]{1,0:T(8,128)(2,1)} %keys.15, bf16[512,1024]{1,0:T(8,128)(2,1)} %values.15, ...), custom_call_target="tpu_custom_call", output_to_operand_aliasing={{}: (14, {})} | custom-call | flops 12000000000 | bytes 8388608 | tf_op jit(solution)/shard_map/attend/pallas_call | solution.py:399
  145.5 1.9 %collective-permute-start.10 = (bf16[4,2,128,128]{3,2,1,0:T(8,128)(2,1)S(1)}, bf16[4,2,128,128]{3,2,1,0:T(8,128)(2,1)S(1)}, u32[]{:S(2)}, u32[]{:S(2)}) collective-permute-start(bf16[4,2,128,128]{3,2,1,0:T(8,128)(2,1)S(1)} %collective-permute-done.9.refs_5_), channel_id=1, source_target_pairs={{0,1},{1,0},{2,3},{3,2},{4,5},{5,4},{6,7},{7,6},{8,9},{9,8},{10,11... | collective-permute-start | bytes 786440 | tf_op jit(solution)/shard_map/ppermute | solution.py:430
  147.9 2.1 %collective-permute-start.14 = (bf16[4,2,128,128]{3,2,1,0:T(8,128)(2,1)S(1)}, bf16[4,2,128,128]{3,2,1,0:T(8,128)(2,1)S(1)}, u32[]{:S(2)}, u32[]{:S(2)}) collective-permute-start(bf16[4,2,128,128]{3,2,1,0:T(8,128)(2,1)S(1)} %collective-permute-done.13.refs_7_), channel_id=1, source_target_pairs={{0,1},{1,0},{2,3},{3,2},{4,5},{5,4},{6,7},{7,6},{8,9},{9,8},{10,11... | collective-permute-start | bytes 786440 | tf_op jit(solution)/shard_map/ppermute | solution.py:430
  150.0 3.5 %collective-permute-done.24.refs_3_ = bf16[4,2,128,128]{3,2,1,0:T(8,128)(2,1)S(1)} collective-permute-done((bf16[4,2,128,128]{3,2,1,0:T(8,128)(2,1)S(1)}, bf16[4,2,128,128]{3,2,1,0:T(8,128)(2,1)S(1)}, u32[]{:S(2)}, u32[]{:S(2)}) %collective-permute-start.24) | collective-permute-done | bytes 262176 | tf_op jit(solution)/shard_map/ppermute | solution.py:430
  154.3 8.1 %attend.8.refs_4_ = bf16[512,5120]{1,0:T(8,128)(2,1)} custom-call(s32[2]{0:T(128)} %pad_add_fusion.place, s32[16,16]{1,0:T(8,128)} %choose.9, s32[16]{0:T(128)} %live.9, bf16[512,5120]{1,0:T(8,128)(2,1)} %queries.9, bf16[512,1024]{1,0:T(8,128)(2,1)} %keys.15, bf16[512,1024]{1,0:T(8,128)(2,1)} %values.15, ...), custom_call_target="tpu_custom_call", output_to_operand_aliasing={{}: (14, {})} | custom-call | flops 12000000000 | bytes 8388608 | tf_op jit(solution)/shard_map/attend/pallas_call | solution.py:399
  163.3 5.6 %collective-permute-done.12.refs_2_ = bf16[4,2,128,128]{3,2,1,0:T(8,128)(2,1)S(1)} collective-permute-done((bf16[4,2,128,128]{3,2,1,0:T(8,128)(2,1)S(1)}, bf16[4,2,128,128]{3,2,1,0:T(8,128)(2,1)S(1)}, u32[]{:S(2)}, u32[]{:S(2)}) %collective-permute-start.12) | collective-permute-done | bytes 262176 | tf_op jit(solution)/shard_map/ppermute | solution.py:430
  169.0 4.7 %collective-permute-done.14.refs_3_ = bf16[4,2,128,128]{3,2,1,0:T(8,128)(2,1)S(1)} collective-permute-done((bf16[4,2,128,128]{3,2,1,0:T(8,128)(2,1)S(1)}, bf16[4,2,128,128]{3,2,1,0:T(8,128)(2,1)S(1)}, u32[]{:S(2)}, u32[]{:S(2)}) %collective-permute-start.14) | collective-permute-done | bytes 262176 | tf_op jit(solution)/shard_map/ppermute | solution.py:430
  174.5 5.5 %attend.9 = bf16[512,5120]{1,0:T(8,128)(2,1)} custom-call(s32[2]{0:T(128)} %pad_add_fusion.place, s32[16,16]{1,0:T(8,128)} %choose.9, s32[16]{0:T(128)} %live.9, bf16[512,5120]{1,0:T(8,128)(2,1)} %queries.9, bf16[512,1024]{1,0:T(8,128)(2,1)} %keys.15, bf16[512,1024]{1,0:T(8,128)(2,1)} %values.15, ...), custom_call_target="tpu_custom_call", output_to_operand_aliasing={{}: (10, {})} | custom-call | flops 6000000000 | bytes 8388608 | tf_op jit(solution)/shard_map/attend/pallas_call | solution.py:399
  (151 shorter events, 15.8 us)
Async XLA Ops:
  1.2 10.2 %collective-permute-start.32 = (bf16[2,512,128]{2,1,0:T(8,128)(2,1)S(1)}, bf16[2,512,128]{2,1,0:T(8,128)(2,1)S(1)}, u32[]{:S(2)}, u32[]{:S(2)}) collective-permute-start(bf16[2,512,128]{2,1,0:T(8,128)(2,1)S(1)} %pad_maximum_fusion.2), channel_id=1, source_target_pairs={{0,1},{1,0},{2,3},{3,2},{4,5},{5,4},{6,7},{7,6},{8,9},{9,8},{10,11... | collective-permute-start | bytes 786440 | tf_op jit(solution)/shard_map/ppermute | solution.py:352
  4.3 22.2 %collective-permute-start.1 = (bf16[2,512,128]{2,1,0:T(8,128)(2,1)S(1)}, bf16[2,512,128]{2,1,0:T(8,128)(2,1)S(1)}, u32[]{:S(2)}, u32[]{:S(2)}) collective-permute-start(bf16[2,512,128]{2,1,0:T(8,128)(2,1)S(1)} %pad_maximum_fusion.1), channel_id=1, source_target_pairs={{0,1},{1,0},{2,3},{3,2},{4,5},{5,4},{6,7},{7,6},{8,9},{9,8},{10,11... | collective-permute-start | bytes 786440 | tf_op jit(solution)/shard_map/ppermute | solution.py:352
  15.3 15.1 %collective-permute-start.33 = (bf16[4,2,128,128]{3,2,1,0:T(8,128)(2,1)}, bf16[4,2,128,128]{3,2,1,0:T(8,128)(2,1)S(1)}, u32[]{:S(2)}, u32[]{:S(2)}) collective-permute-start(bf16[4,2,128,128]{3,2,1,0:T(8,128)(2,1)} %get-tuple-element.62), channel_id=1, source_target_pairs={{0,8},{2,10},{4,12},{6,14},{8,16},{10,18},{12,20},{14,22},{16,24},... | collective-permute-start | bytes 786440 | tf_op jit(solution)/shard_map/ppermute | solution.py:420
  19.2 12.7 %collective-permute-start.34 = (bf16[4,2,128,128]{3,2,1,0:T(8,128)(2,1)}, bf16[4,2,128,128]{3,2,1,0:T(8,128)(2,1)S(1)}, u32[]{:S(2)}, u32[]{:S(2)}) collective-permute-start(bf16[4,2,128,128]{3,2,1,0:T(8,128)(2,1)} %get-tuple-element.63), channel_id=1, source_target_pairs={{0,16},{2,18},{4,20},{6,22},{8,24},{10,26},{12,28},{14,30},{1,17},... | collective-permute-start | bytes 786440 | tf_op jit(solution)/shard_map/ppermute | solution.py:420
  23.6 25.2 %collective-permute-start = (bf16[2,512,256]{2,1,0:T(8,128)(2,1)S(1)}, bf16[2,512,256]{2,1,0:T(8,128)(2,1)S(1)}, u32[]{:S(2)}, u32[]{:S(2)}) collective-permute-start(bf16[2,512,256]{2,1,0:T(8,128)(2,1)S(1)} %pad_maximum_fusion), channel_id=1, source_target_pairs={{0,1},{1,0},{2,3},{3,2},{4,5},{5,4},{6,7},{7,6},{8,9},{9,8},{10,11... | collective-permute-start | bytes 1572872 | tf_op jit(solution)/shard_map/ppermute | solution.py:352
  25.2 9.5 %collective-permute-start.35 = (bf16[4,2,128,128]{3,2,1,0:T(8,128)(2,1)}, bf16[4,2,128,128]{3,2,1,0:T(8,128)(2,1)S(1)}, u32[]{:S(2)}, u32[]{:S(2)}) collective-permute-start(bf16[4,2,128,128]{3,2,1,0:T(8,128)(2,1)} %get-tuple-element.64), channel_id=1, source_target_pairs={{0,24},{2,26},{4,28},{6,30},{1,25},{3,27},{5,29},{7,31}} | collective-permute-start | bytes 786440 | tf_op jit(solution)/shard_map/ppermute | solution.py:420
  30.3 7.8 %collective-permute-start.2 = (bf16[4,2,128,128]{3,2,1,0:T(8,128)(2,1)}, bf16[4,2,128,128]{3,2,1,0:T(8,128)(2,1)S(1)}, u32[]{:S(2)}, u32[]{:S(2)}) collective-permute-start(bf16[4,2,128,128]{3,2,1,0:T(8,128)(2,1)} %get-tuple-element.38), channel_id=1, source_target_pairs={{0,2},{2,0},{4,6},{6,4},{8,10},{10,8},{12,14},{14,12},{16,18},{18,... | collective-permute-start | bytes 786440 | tf_op jit(solution)/shard_map/ppermute | solution.py:425
  30.4 9.4 %collective-permute-start.3 = (bf16[4,2,128,128]{3,2,1,0:T(8,128)(2,1)}, bf16[4,2,128,128]{3,2,1,0:T(8,128)(2,1)S(1)}, u32[]{:S(2)}, u32[]{:S(2)}) collective-permute-start(bf16[4,2,128,128]{3,2,1,0:T(8,128)(2,1)} %get-tuple-element.39), channel_id=1, source_target_pairs={{0,4},{2,6},{4,0},{6,2},{8,12},{10,14},{12,8},{14,10},{16,20},{18,... | collective-permute-start | bytes 786440 | tf_op jit(solution)/shard_map/ppermute | solution.py:425
  31.9 12.6 %collective-permute-start.4 = (bf16[4,2,128,128]{3,2,1,0:T(8,128)(2,1)}, bf16[4,2,128,128]{3,2,1,0:T(8,128)(2,1)S(1)}, u32[]{:S(2)}, u32[]{:S(2)}) collective-permute-start(bf16[4,2,128,128]{3,2,1,0:T(8,128)(2,1)} %get-tuple-element.40), channel_id=1, source_target_pairs={{0,6},{2,4},{4,2},{6,0},{8,14},{10,12},{12,10},{14,8},{16,22},{18,... | collective-permute-start | bytes 786440 | tf_op jit(solution)/shard_map/ppermute | solution.py:425
  38.1 25.1 %collective-permute-start.37 = (bf16[4,2,128,128]{3,2,1,0:T(8,128)(2,1)}, bf16[4,2,128,128]{3,2,1,0:T(8,128)(2,1)S(1)}, u32[]{:S(2)}, u32[]{:S(2)}) collective-permute-start(bf16[4,2,128,128]{3,2,1,0:T(8,128)(2,1)} %get-tuple-element.66), channel_id=1, source_target_pairs={{0,2},{2,0},{4,6},{6,4},{8,10},{10,8},{12,14},{14,12},{16,18},{18,... | collective-permute-start | bytes 786440 | tf_op jit(solution)/shard_map/ppermute | solution.py:425
  38.2 26.1 %collective-permute-start.39 = (bf16[4,2,128,128]{3,2,1,0:T(8,128)(2,1)}, bf16[4,2,128,128]{3,2,1,0:T(8,128)(2,1)S(1)}, u32[]{:S(2)}, u32[]{:S(2)}) collective-permute-start(bf16[4,2,128,128]{3,2,1,0:T(8,128)(2,1)} %get-tuple-element.67), channel_id=1, source_target_pairs={{0,4},{2,6},{4,0},{6,2},{8,12},{10,14},{12,8},{14,10},{16,20},{18,... | collective-permute-start | bytes 786440 | tf_op jit(solution)/shard_map/ppermute | solution.py:425
  39.8 14.7 %collective-permute-start.36 = (bf16[3,2,128,128]{3,2,1,0:T(8,128)(2,1)}, bf16[3,2,128,128]{3,2,1,0:T(8,128)(2,1)S(1)}, u32[]{:S(2)}, u32[]{:S(2)}) collective-permute-start(bf16[3,2,128,128]{3,2,1,0:T(8,128)(2,1)} %get-tuple-element.65.refs_0_), channel_id=1, source_target_pairs={{0,1},{1,0},{2,3},{3,2},{4,5},{5,4},{6,7},{7,6},{8,9},{9,8},{10,11... | collective-permute-start | bytes 589832 | tf_op jit(solution)/shard_map/ppermute | solution.py:430
  48.2 14.9 %collective-permute-start.25 = (bf16[3,2,128,128]{3,2,1,0:T(8,128)(2,1)}, bf16[3,2,128,128]{3,2,1,0:T(8,128)(2,1)S(1)}, u32[]{:S(2)}, u32[]{:S(2)}) collective-permute-start(bf16[3,2,128,128]{3,2,1,0:T(8,128)(2,1)} %get-tuple-element.41.refs_1_.refs_4_), channel_id=1, source_target_pairs={{0,1},{1,0},{2,3},{3,2},{4,5},{5,4},{6,7},{7,6},{8,9},{9,8},{10,11... | collective-permute-start | bytes 589832 | tf_op jit(solution)/shard_map/ppermute | solution.py:430
  48.8 16.4 %collective-permute-start.41 = (bf16[4,2,128,128]{3,2,1,0:T(8,128)(2,1)}, bf16[4,2,128,128]{3,2,1,0:T(8,128)(2,1)S(1)}, u32[]{:S(2)}, u32[]{:S(2)}) collective-permute-start(bf16[4,2,128,128]{3,2,1,0:T(8,128)(2,1)} %get-tuple-element.68), channel_id=1, source_target_pairs={{0,6},{2,4},{4,2},{6,0},{8,14},{10,12},{12,10},{14,8},{16,22},{18,... | collective-permute-start | bytes 786440 | tf_op jit(solution)/shard_map/ppermute | solution.py:425
  54.5 16.3 %collective-permute-start.26 = (bf16[4,2,128,128]{3,2,1,0:T(8,128)(2,1)}, bf16[4,2,128,128]{3,2,1,0:T(8,128)(2,1)S(1)}, u32[]{:S(2)}, u32[]{:S(2)}) collective-permute-start(bf16[4,2,128,128]{3,2,1,0:T(8,128)(2,1)} %get-tuple-element.58), channel_id=1, source_target_pairs={{0,8},{2,10},{4,12},{6,14},{8,16},{10,18},{12,20},{14,22},{16,24},... | collective-permute-start | bytes 786440 | tf_op jit(solution)/shard_map/ppermute | solution.py:420
  63.1 12.7 %collective-permute-start.15 = (bf16[4,2,128,128]{3,2,1,0:T(8,128)(2,1)}, bf16[4,2,128,128]{3,2,1,0:T(8,128)(2,1)S(1)}, u32[]{:S(2)}, u32[]{:S(2)}) collective-permute-start(bf16[4,2,128,128]{3,2,1,0:T(8,128)(2,1)} %get-tuple-element.51), channel_id=1, source_target_pairs={{0,2},{2,0},{4,6},{6,4},{8,10},{10,8},{12,14},{14,12},{16,18},{18,... | collective-permute-start | bytes 786440 | tf_op jit(solution)/shard_map/ppermute | solution.py:425
  63.8 36.8 %copy-start.17 = (bf16[4,2,128,128]{3,2,1,0:T(8,128)(2,1)}, bf16[4,2,128,128]{3,2,1,0:T(8,128)(2,1)S(1)}, u32[]{:S(2)}) copy-start(bf16[4,2,128,128]{3,2,1,0:T(8,128)(2,1)S(1)} %collective-permute-done.37.refs_1_) | copy-start | bytes 786436
  63.8 12.1 %collective-permute-start.16 = (bf16[4,2,128,128]{3,2,1,0:T(8,128)(2,1)}, bf16[4,2,128,128]{3,2,1,0:T(8,128)(2,1)S(1)}, u32[]{:S(2)}, u32[]{:S(2)}) collective-permute-start(bf16[4,2,128,128]{3,2,1,0:T(8,128)(2,1)} %get-tuple-element.52), channel_id=1, source_target_pairs={{0,4},{2,6},{4,0},{6,2},{8,12},{10,14},{12,8},{14,10},{16,20},{18,... | collective-permute-start | bytes 786440 | tf_op jit(solution)/shard_map/ppermute | solution.py:425
  64.3 36.3 %copy-start.16 = (bf16[4,2,128,128]{3,2,1,0:T(8,128)(2,1)}, bf16[4,2,128,128]{3,2,1,0:T(8,128)(2,1)S(1)}, u32[]{:S(2)}) copy-start(bf16[4,2,128,128]{3,2,1,0:T(8,128)(2,1)S(1)} %collective-permute-done.39.refs_2_) | copy-start | bytes 786436
  64.3 12.9 %collective-permute-start.17 = (bf16[4,2,128,128]{3,2,1,0:T(8,128)(2,1)}, bf16[4,2,128,128]{3,2,1,0:T(8,128)(2,1)S(1)}, u32[]{:S(2)}, u32[]{:S(2)}) collective-permute-start(bf16[4,2,128,128]{3,2,1,0:T(8,128)(2,1)} %get-tuple-element.53), channel_id=1, source_target_pairs={{0,6},{2,4},{4,2},{6,0},{8,14},{10,12},{12,10},{14,8},{16,22},{18,... | collective-permute-start | bytes 786440 | tf_op jit(solution)/shard_map/ppermute | solution.py:425
  65.2 35.4 %copy-start.19 = (bf16[4,2,128,128]{3,2,1,0:T(8,128)(2,1)}, bf16[4,2,128,128]{3,2,1,0:T(8,128)(2,1)S(1)}, u32[]{:S(2)}) copy-start(bf16[4,2,128,128]{3,2,1,0:T(8,128)(2,1)S(1)} %collective-permute-done.41.refs_3_) | copy-start | bytes 786436
  65.2 15.9 %collective-permute-start.28 = (bf16[4,2,128,128]{3,2,1,0:T(8,128)(2,1)}, bf16[4,2,128,128]{3,2,1,0:T(8,128)(2,1)S(1)}, u32[]{:S(2)}, u32[]{:S(2)}) collective-permute-start(bf16[4,2,128,128]{3,2,1,0:T(8,128)(2,1)} %get-tuple-element.59), channel_id=1, source_target_pairs={{0,16},{2,18},{4,20},{6,22},{8,24},{10,26},{12,28},{14,30},{1,17},... | collective-permute-start | bytes 786440 | tf_op jit(solution)/shard_map/ppermute | solution.py:420
  70.9 48.6 %copy-start.18 = (bf16[4,2,128,128]{3,2,1,0:T(8,128)(2,1)}, bf16[4,2,128,128]{3,2,1,0:T(8,128)(2,1)S(1)}, u32[]{:S(2)}) copy-start(bf16[4,2,128,128]{3,2,1,0:T(8,128)(2,1)S(1)} %collective-permute-done.26.refs_5_) | copy-start | bytes 786436
  70.9 12.5 %collective-permute-start.30 = (bf16[4,2,128,128]{3,2,1,0:T(8,128)(2,1)}, bf16[4,2,128,128]{3,2,1,0:T(8,128)(2,1)S(1)}, u32[]{:S(2)}, u32[]{:S(2)}) collective-permute-start(bf16[4,2,128,128]{3,2,1,0:T(8,128)(2,1)} %get-tuple-element.60), channel_id=1, source_target_pairs={{0,24},{2,26},{4,28},{6,30},{1,25},{3,27},{5,29},{7,31}} | collective-permute-start | bytes 786440 | tf_op jit(solution)/shard_map/ppermute | solution.py:420
  75.8 15.8 %collective-permute-start.5 = (bf16[4,2,128,128]{3,2,1,0:T(8,128)(2,1)}, bf16[4,2,128,128]{3,2,1,0:T(8,128)(2,1)S(1)}, u32[]{:S(2)}, u32[]{:S(2)}) collective-permute-start(bf16[4,2,128,128]{3,2,1,0:T(8,128)(2,1)} %get-tuple-element.43), channel_id=1, source_target_pairs={{0,2},{2,0},{4,6},{6,4},{8,10},{10,8},{12,14},{14,12},{16,18},{18,... | collective-permute-start | bytes 786440 | tf_op jit(solution)/shard_map/ppermute | solution.py:425
  75.9 21.0 %collective-permute-start.6 = (bf16[4,2,128,128]{3,2,1,0:T(8,128)(2,1)}, bf16[4,2,128,128]{3,2,1,0:T(8,128)(2,1)S(1)}, u32[]{:S(2)}, u32[]{:S(2)}) collective-permute-start(bf16[4,2,128,128]{3,2,1,0:T(8,128)(2,1)} %get-tuple-element.44), channel_id=1, source_target_pairs={{0,4},{2,6},{4,0},{6,2},{8,12},{10,14},{12,8},{14,10},{16,20},{18,... | collective-permute-start | bytes 786440 | tf_op jit(solution)/shard_map/ppermute | solution.py:425
  77.2 21.3 %collective-permute-start.7 = (bf16[4,2,128,128]{3,2,1,0:T(8,128)(2,1)}, bf16[4,2,128,128]{3,2,1,0:T(8,128)(2,1)S(1)}, u32[]{:S(2)}, u32[]{:S(2)}) collective-permute-start(bf16[4,2,128,128]{3,2,1,0:T(8,128)(2,1)} %get-tuple-element.45), channel_id=1, source_target_pairs={{0,6},{2,4},{4,2},{6,0},{8,14},{10,12},{12,10},{14,8},{16,22},{18,... | collective-permute-start | bytes 786440 | tf_op jit(solution)/shard_map/ppermute | solution.py:425
  81.1 36.3 %copy-start.20 = (bf16[4,2,128,128]{3,2,1,0:T(8,128)(2,1)}, bf16[4,2,128,128]{3,2,1,0:T(8,128)(2,1)S(1)}, u32[]{:S(2)}) copy-start(bf16[4,2,128,128]{3,2,1,0:T(8,128)(2,1)S(1)} %collective-permute-done.28.refs_6_) | copy-start | bytes 786436
  81.1 18.0 %collective-permute-start.18 = (bf16[3,2,128,128]{3,2,1,0:T(8,128)(2,1)}, bf16[3,2,128,128]{3,2,1,0:T(8,128)(2,1)S(1)}, u32[]{:S(2)}, u32[]{:S(2)}) collective-permute-start(bf16[3,2,128,128]{3,2,1,0:T(8,128)(2,1)} %get-tuple-element.54.refs_4_), channel_id=1, source_target_pairs={{0,1},{1,0},{2,3},{3,2},{4,5},{5,4},{6,7},{7,6},{8,9},{9,8},{10,11... | collective-permute-start | bytes 589832 | tf_op jit(solution)/shard_map/ppermute | solution.py:430
  83.4 34.0 %collective-permute-start.19 = (bf16[4,2,128,128]{3,2,1,0:T(8,128)(2,1)}, bf16[4,2,128,128]{3,2,1,0:T(8,128)(2,1)S(1)}, u32[]{:S(2)}, u32[]{:S(2)}) collective-permute-start(bf16[4,2,128,128]{3,2,1,0:T(8,128)(2,1)} %get-tuple-element.55), channel_id=1, source_target_pairs={{0,8},{2,10},{4,12},{6,14},{8,16},{10,18},{12,20},{14,22},{16,24},... | collective-permute-start | bytes 786440 | tf_op jit(solution)/shard_map/ppermute | solution.py:420
  91.6 26.3 %collective-permute-start.21 = (bf16[4,2,128,128]{3,2,1,0:T(8,128)(2,1)}, bf16[4,2,128,128]{3,2,1,0:T(8,128)(2,1)S(1)}, u32[]{:S(2)}, u32[]{:S(2)}) collective-permute-start(bf16[4,2,128,128]{3,2,1,0:T(8,128)(2,1)} %get-tuple-element.56), channel_id=1, source_target_pairs={{0,16},{2,18},{4,20},{6,22},{8,24},{10,26},{12,28},{14,30},{1,17},... | collective-permute-start | bytes 786440 | tf_op jit(solution)/shard_map/ppermute | solution.py:420
  96.9 12.2 %collective-permute-start.38 = (bf16[4,2,128,128]{3,2,1,0:T(8,128)(2,1)S(1)}, bf16[4,2,128,128]{3,2,1,0:T(8,128)(2,1)S(1)}, u32[]{:S(2)}, u32[]{:S(2)}) collective-permute-start(bf16[4,2,128,128]{3,2,1,0:T(8,128)(2,1)S(1)} %collective-permute-done.37.refs_1_), channel_id=1, source_target_pairs={{0,1},{1,0},{2,3},{3,2},{4,5},{5,4},{6,7},{7,6},{8,9},{9,8},{10,11... | collective-permute-start | bytes 786440 | tf_op jit(solution)/shard_map/ppermute | solution.py:430
  98.5 13.3 %collective-permute-start.40 = (bf16[4,2,128,128]{3,2,1,0:T(8,128)(2,1)S(1)}, bf16[4,2,128,128]{3,2,1,0:T(8,128)(2,1)S(1)}, u32[]{:S(2)}, u32[]{:S(2)}) collective-permute-start(bf16[4,2,128,128]{3,2,1,0:T(8,128)(2,1)S(1)} %collective-permute-done.39.refs_2_), channel_id=1, source_target_pairs={{0,1},{1,0},{2,3},{3,2},{4,5},{5,4},{6,7},{7,6},{8,9},{9,8},{10,11... | collective-permute-start | bytes 786440 | tf_op jit(solution)/shard_map/ppermute | solution.py:430
  99.1 16.8 %collective-permute-start.42 = (bf16[4,2,128,128]{3,2,1,0:T(8,128)(2,1)S(1)}, bf16[4,2,128,128]{3,2,1,0:T(8,128)(2,1)}, u32[]{:S(2)}, u32[]{:S(2)}) collective-permute-start(bf16[4,2,128,128]{3,2,1,0:T(8,128)(2,1)S(1)} %collective-permute-done.41.refs_3_), channel_id=1, source_target_pairs={{0,1},{1,0},{2,3},{3,2},{4,5},{5,4},{6,7},{7,6},{8,9},{9,8},{10,11... | collective-permute-start | bytes 786440 | tf_op jit(solution)/shard_map/ppermute | solution.py:430
  109.1 18.5 %collective-permute-start.23 = (bf16[4,2,128,128]{3,2,1,0:T(8,128)(2,1)S(1)}, bf16[4,2,128,128]{3,2,1,0:T(8,128)(2,1)S(1)}, u32[]{:S(2)}, u32[]{:S(2)}) collective-permute-start(bf16[4,2,128,128]{3,2,1,0:T(8,128)(2,1)S(1)} %copy-done.26), channel_id=1, source_target_pairs={{0,24},{2,26},{4,28},{6,30},{1,25},{3,27},{5,29},{7,31}} | collective-permute-start | bytes 786440 | tf_op jit(solution)/shard_map/ppermute | solution.py:420
  111.9 23.4 %collective-permute-start.11 = (bf16[4,2,128,128]{3,2,1,0:T(8,128)(2,1)}, bf16[4,2,128,128]{3,2,1,0:T(8,128)(2,1)S(1)}, u32[]{:S(2)}, u32[]{:S(2)}) collective-permute-start(bf16[4,2,128,128]{3,2,1,0:T(8,128)(2,1)} %get-tuple-element.48), channel_id=1, source_target_pairs={{0,16},{2,18},{4,20},{6,22},{8,24},{10,26},{12,28},{14,30},{1,17},... | collective-permute-start | bytes 786440 | tf_op jit(solution)/shard_map/ppermute | solution.py:420
  115.8 13.3 %collective-permute-start.27 = (bf16[4,2,128,128]{3,2,1,0:T(8,128)(2,1)S(1)}, bf16[4,2,128,128]{3,2,1,0:T(8,128)(2,1)S(1)}, u32[]{:S(2)}, u32[]{:S(2)}) collective-permute-start(bf16[4,2,128,128]{3,2,1,0:T(8,128)(2,1)S(1)} %collective-permute-done.26.refs_5_), channel_id=1, source_target_pairs={{0,1},{1,0},{2,3},{3,2},{4,5},{5,4},{6,7},{7,6},{8,9},{9,8},{10,11... | collective-permute-start | bytes 786440 | tf_op jit(solution)/shard_map/ppermute | solution.py:430
  117.4 15.0 %collective-permute-start.29 = (bf16[4,2,128,128]{3,2,1,0:T(8,128)(2,1)S(1)}, bf16[4,2,128,128]{3,2,1,0:T(8,128)(2,1)S(1)}, u32[]{:S(2)}, u32[]{:S(2)}) collective-permute-start(bf16[4,2,128,128]{3,2,1,0:T(8,128)(2,1)S(1)} %collective-permute-done.28.refs_6_), channel_id=1, source_target_pairs={{0,1},{1,0},{2,3},{3,2},{4,5},{5,4},{6,7},{7,6},{8,9},{9,8},{10,11... | collective-permute-start | bytes 786440 | tf_op jit(solution)/shard_map/ppermute | solution.py:430
  117.9 17.2 %collective-permute-start.31 = (bf16[4,2,128,128]{3,2,1,0:T(8,128)(2,1)S(1)}, bf16[4,2,128,128]{3,2,1,0:T(8,128)(2,1)}, u32[]{:S(2)}, u32[]{:S(2)}) collective-permute-start(bf16[4,2,128,128]{3,2,1,0:T(8,128)(2,1)S(1)} %collective-permute-done.30.refs_7_), channel_id=1, source_target_pairs={{0,1},{1,0},{2,3},{3,2},{4,5},{5,4},{6,7},{7,6},{8,9},{9,8},{10,11... | collective-permute-start | bytes 786440 | tf_op jit(solution)/shard_map/ppermute | solution.py:430
  127.7 17.6 %collective-permute-start.13 = (bf16[4,2,128,128]{3,2,1,0:T(8,128)(2,1)S(1)}, bf16[4,2,128,128]{3,2,1,0:T(8,128)(2,1)S(1)}, u32[]{:S(2)}, u32[]{:S(2)}) collective-permute-start(bf16[4,2,128,128]{3,2,1,0:T(8,128)(2,1)S(1)} %copy-done.28), channel_id=1, source_target_pairs={{0,24},{2,26},{4,28},{6,30},{1,25},{3,27},{5,29},{7,31}} | collective-permute-start | bytes 786440 | tf_op jit(solution)/shard_map/ppermute | solution.py:420
  129.2 16.3 %collective-permute-start.9 = (bf16[4,2,128,128]{3,2,1,0:T(8,128)(2,1)S(1)}, bf16[4,2,128,128]{3,2,1,0:T(8,128)(2,1)S(1)}, u32[]{:S(2)}, u32[]{:S(2)}) collective-permute-start(bf16[4,2,128,128]{3,2,1,0:T(8,128)(2,1)S(1)} %copy-done.27), channel_id=1, source_target_pairs={{0,8},{2,10},{4,12},{6,14},{8,16},{10,18},{12,20},{14,22},{16,24},... | collective-permute-start | bytes 786440 | tf_op jit(solution)/shard_map/ppermute | solution.py:420
  132.4 15.0 %collective-permute-start.20 = (bf16[4,2,128,128]{3,2,1,0:T(8,128)(2,1)S(1)}, bf16[4,2,128,128]{3,2,1,0:T(8,128)(2,1)S(1)}, u32[]{:S(2)}, u32[]{:S(2)}) collective-permute-start(bf16[4,2,128,128]{3,2,1,0:T(8,128)(2,1)S(1)} %collective-permute-done.19.refs_5_), channel_id=1, source_target_pairs={{0,1},{1,0},{2,3},{3,2},{4,5},{5,4},{6,7},{7,6},{8,9},{9,8},{10,11... | collective-permute-start | bytes 786440 | tf_op jit(solution)/shard_map/ppermute | solution.py:430
  135.1 12.8 %collective-permute-start.22 = (bf16[4,2,128,128]{3,2,1,0:T(8,128)(2,1)S(1)}, bf16[4,2,128,128]{3,2,1,0:T(8,128)(2,1)S(1)}, u32[]{:S(2)}, u32[]{:S(2)}) collective-permute-start(bf16[4,2,128,128]{3,2,1,0:T(8,128)(2,1)S(1)} %collective-permute-done.21.refs_6_), channel_id=1, source_target_pairs={{0,1},{1,0},{2,3},{3,2},{4,5},{5,4},{6,7},{7,6},{8,9},{9,8},{10,11... | collective-permute-start | bytes 786440 | tf_op jit(solution)/shard_map/ppermute | solution.py:430
  135.3 18.2 %collective-permute-start.24 = (bf16[4,2,128,128]{3,2,1,0:T(8,128)(2,1)S(1)}, bf16[4,2,128,128]{3,2,1,0:T(8,128)(2,1)S(1)}, u32[]{:S(2)}, u32[]{:S(2)}) collective-permute-start(bf16[4,2,128,128]{3,2,1,0:T(8,128)(2,1)S(1)} %collective-permute-done.23.refs_7_), channel_id=1, source_target_pairs={{0,1},{1,0},{2,3},{3,2},{4,5},{5,4},{6,7},{7,6},{8,9},{9,8},{10,11... | collective-permute-start | bytes 786440 | tf_op jit(solution)/shard_map/ppermute | solution.py:430
  145.3 17.1 %collective-permute-start.8 = (bf16[3,2,128,128]{3,2,1,0:T(8,128)(2,1)S(1)}, bf16[3,2,128,128]{3,2,1,0:T(8,128)(2,1)S(1)}, u32[]{:S(2)}, u32[]{:S(2)}) collective-permute-start(bf16[3,2,128,128]{3,2,1,0:T(8,128)(2,1)S(1)} %copy-done.44), channel_id=1, source_target_pairs={{0,1},{1,0},{2,3},{3,2},{4,5},{5,4},{6,7},{7,6},{8,9},{9,8},{10,11... | collective-permute-start | bytes 589832 | tf_op jit(solution)/shard_map/ppermute | solution.py:430
  145.5 17.8 %collective-permute-start.10 = (bf16[4,2,128,128]{3,2,1,0:T(8,128)(2,1)S(1)}, bf16[4,2,128,128]{3,2,1,0:T(8,128)(2,1)S(1)}, u32[]{:S(2)}, u32[]{:S(2)}) collective-permute-start(bf16[4,2,128,128]{3,2,1,0:T(8,128)(2,1)S(1)} %collective-permute-done.9.refs_5_), channel_id=1, source_target_pairs={{0,1},{1,0},{2,3},{3,2},{4,5},{5,4},{6,7},{7,6},{8,9},{9,8},{10,11... | collective-permute-start | bytes 786440 | tf_op jit(solution)/shard_map/ppermute | solution.py:430
  147.4 21.5 %collective-permute-start.12 = (bf16[4,2,128,128]{3,2,1,0:T(8,128)(2,1)S(1)}, bf16[4,2,128,128]{3,2,1,0:T(8,128)(2,1)S(1)}, u32[]{:S(2)}, u32[]{:S(2)}) collective-permute-start(bf16[4,2,128,128]{3,2,1,0:T(8,128)(2,1)S(1)} %collective-permute-done.11.refs_6_), channel_id=1, source_target_pairs={{0,1},{1,0},{2,3},{3,2},{4,5},{5,4},{6,7},{7,6},{8,9},{9,8},{10,11... | collective-permute-start | bytes 786440 | tf_op jit(solution)/shard_map/ppermute | solution.py:430
  147.9 25.8 %collective-permute-start.14 = (bf16[4,2,128,128]{3,2,1,0:T(8,128)(2,1)S(1)}, bf16[4,2,128,128]{3,2,1,0:T(8,128)(2,1)S(1)}, u32[]{:S(2)}, u32[]{:S(2)}) collective-permute-start(bf16[4,2,128,128]{3,2,1,0:T(8,128)(2,1)S(1)} %collective-permute-done.13.refs_7_), channel_id=1, source_target_pairs={{0,1},{1,0},{2,3},{3,2},{4,5},{5,4},{6,7},{7,6},{8,9},{9,8},{10,11... | collective-permute-start | bytes 786440 | tf_op jit(solution)/shard_map/ppermute | solution.py:430
  (41 other events, 322.5 us)
